TPU v7x, 32 devices: a whole 2x2x4 slice. The times are simulated.
32 devices in a mesh: row: 4 (over y, core), col: 8 (over z, x).
Axes of the slice: x: 2, y: 2, z: 4, core: 2. Of those that a mesh axis runs over, the one named last changes fastest.
Arguments:
- features: bfloat16 [4096, 128], P(('row', 'col')), may hold values from -6 to 6
- norm_weight: float32 [4096], P(('row', 'col')), may hold values from 0.01767767 to 0.110485435
- weight_in: bfloat16 [128, 256], replicated, may hold values from -6 to 6
- weight_out: bfloat16 [256, 128], replicated, may hold values from -6 to 6
- labels: int32 [4096], P(('row', 'col')), may hold values from 0 to 127
- tile_slot: int32 [32, 128], P(('row', 'col')), may hold values from 0 to 31
- tile_edges: int32 [32, 128, 2, 512], P(('row', 'col')), may hold values from 0 to 127
- tile_count: int32 [32], P(('row', 'col')), may hold values from 32 to 128, as said below
Outputs:
- grad_in: float32 [128, 256], replicated
- grad_out: float32 [256, 128], replicated
- loss: float32 [], replicated
Inputs may be any that keep to these rules, and one draw needn't show every extreme that they name: `tile_slot`: position p of a slot covers the tile whose target rows start at 128 * (p // 4) and whose source columns start at 128 * (p % 4) within the device's block; a position may occur in several slots. Entry k of a slot marks row tile_edges[s, 0, k] and column tile_edges[s, 1, k] of its slot's tile; repeated entries count again. `tile_count`: slots at and after this number are not live; in every draw some device has all 128 slots live and another device only 32.
All inputs are finite; a program needn't handle non-finite values.
Results may differ from a plain program's by a relative error of at most 0.0084.
Values may be sent and summed in bfloat16 or wider, within the bound.
A program may use at most 64 MiB of HBM per device.

v0:
```python
import jax
import jax.numpy as jnp
from jax import lax
from jax.sharding import PartitionSpec as P

TILE = 128
SOFTCAP = 15.0
LOSS_SCALE = 1024.0
HIGHEST = lax.Precision.HIGHEST
CONTRACT_ROWS = (((0,), (0,)), ((), ()))


def densify(tile_slot, tile_edges, tile_count, row_group, col_group):
    tile_side = TILE
    col_tiles = col_group // tile_side
    row_tiles = row_group // tile_side
    slot_total = tile_slot.shape[0]
    offsets = jnp.arange(tile_side, dtype=jnp.int32)
    row_onehot = (tile_edges[:, 0, :, None] == offsets[None, None, :]).astype(jnp.bfloat16)
    col_onehot = (tile_edges[:, 1, :, None] == offsets[None, None, :]).astype(jnp.bfloat16)
    slot_tiles = jnp.einsum(
        "ser,sec->src", row_onehot, col_onehot, preferred_element_type=jnp.float32
    )
    slot_tiles = slot_tiles.astype(jnp.bfloat16).reshape(slot_total, tile_side * tile_side)
    slot_live = jnp.arange(slot_total, dtype=jnp.int32) < tile_count
    places = jnp.arange(row_tiles * col_tiles, dtype=jnp.int32)
    place_onehot = ((tile_slot[:, None] == places[None, :]) & slot_live[:, None]).astype(
        jnp.bfloat16
    )
    placed = lax.dot_general(
        place_onehot, slot_tiles, CONTRACT_ROWS, preferred_element_type=jnp.float32
    )
    placed = placed.astype(jnp.bfloat16).reshape(row_tiles, col_tiles, tile_side, tile_side)
    return placed.transpose(0, 2, 1, 3).reshape(row_group, col_group)


def gather_targets(values):
    return lax.all_gather(values, "col", axis=0, tiled=True)


def sum_sources(partial_sums):
    return lax.psum_scatter(partial_sums, "row", scatter_dimension=0, tiled=True)


def per_device(
    features, norm_weight, weight_in, weight_out, labels, tile_slot, tile_edges, tile_count
):
    row_size = lax.axis_size("row")
    col_size = lax.axis_size("col")
    node_rows = features.shape[0]
    total_nodes = node_rows * row_size * col_size
    adjacency = densify(
        tile_slot[0], tile_edges[0], tile_count[0], node_rows * col_size, node_rows * row_size
    )
    node_scale = norm_weight[:, None]
    normed = (node_scale * features.astype(jnp.float32)).astype(jnp.bfloat16)
    source_one = jnp.dot(normed, weight_in, preferred_element_type=jnp.float32)
    gathered_one = lax.all_gather(source_one, "row", axis=0, tiled=True)
    forward_one = jnp.dot(adjacency.astype(jnp.float32), gathered_one, precision=HIGHEST)
    projected = lax.psum_scatter(forward_one, "col", scatter_dimension=0, tiled=True)
    pre_hidden = node_scale * (projected + source_one)
    hidden = jax.nn.relu(pre_hidden).astype(jnp.bfloat16)
    source_two = (
        node_scale * jnp.dot(hidden, weight_out, preferred_element_type=jnp.float32)
    ).astype(jnp.bfloat16)
    gathered_two = lax.all_gather(source_two, "row", axis=0, tiled=True)
    forward_two = jnp.dot(adjacency, gathered_two, preferred_element_type=jnp.float32)
    logits = node_scale * (
        lax.psum_scatter(forward_two, "col", scatter_dimension=0, tiled=True)
        + source_two.astype(jnp.float32)
    )
    capped = SOFTCAP * jnp.tanh(logits / SOFTCAP)
    exp_capped = jnp.exp(capped)
    exp_total = jnp.sum(exp_capped, axis=1, keepdims=True)
    one_hot = (labels[:, None] == jnp.arange(capped.shape[1], dtype=jnp.int32)[None, :]).astype(
        jnp.float32
    )
    loss_local = jnp.sum(jnp.log(exp_total[:, 0]) - jnp.sum(capped * one_hot, axis=1))
    d_logits = (
        LOSS_SCALE
        / total_nodes
        * (exp_capped / exp_total - one_hot)
        * (1.0 - (capped / SOFTCAP) ** 2)
    )
    back_two = (node_scale * d_logits).astype(jnp.bfloat16)
    backward_two = lax.dot_general(
        adjacency, gather_targets(back_two), CONTRACT_ROWS, preferred_element_type=jnp.float32
    )
    d_source_two = node_scale * (sum_sources(backward_two) + back_two.astype(jnp.float32))
    grad_out_local = lax.dot_general(
        hidden.astype(jnp.float32), d_source_two, CONTRACT_ROWS, precision=HIGHEST
    )
    d_hidden = lax.dot_general(
        d_source_two, weight_out.astype(jnp.float32), (((1,), (1,)), ((), ())), precision=HIGHEST
    )
    back_one = (node_scale * jnp.where(pre_hidden > 0, d_hidden, 0.0)).astype(jnp.bfloat16)
    gathered_back = gather_targets(back_one)
    backward_one = lax.dot_general(
        adjacency, gathered_back, CONTRACT_ROWS, preferred_element_type=jnp.float32
    )
    d_source_one = sum_sources(backward_one) + back_one.astype(jnp.float32)
    grad_in_local = lax.dot_general(
        normed.astype(jnp.float32), d_source_one, CONTRACT_ROWS, precision=HIGHEST
    )
    grad_in, grad_out, loss_sum = lax.psum(
        (grad_in_local, grad_out_local, loss_local), ("row", "col")
    )
    return (grad_in, grad_out, loss_sum / total_nodes)


def solution(mesh):
    in_specs = (
        P(("row", "col"), None),
        P(("row", "col")),
        P(),
        P(),
        P(("row", "col")),
        P(("row", "col"), None),
        P(("row", "col"), None, None, None),
        P(("row", "col")),
    )
    out_specs = (P(), P(), P())
    return jax.shard_map(
        per_device, mesh=mesh, in_specs=in_specs, out_specs=out_specs, check_vma=False
    )
```

profile of v0, /device:TPU:0, one launch (start us, length us, event | category | flops | bytes accessed | tf_op | source)
XLA Modules:
  0.0 426.0 jit_solution(7901533714446784060)
XLA Ops:
  7.2 1.7 fusion.37
  9.0 7.9 %iota_compare_fusion.17 = pred[128,512,128]{1,2,0:T(32,128)(4,1)} fusion(s32[128,512]{1,0:T(8,128)S(1)} %get-tuple-element.10), kind=kLoop, calls=%fused_computation.1.clone.clone.clone.clone.2 | loop fusion | flops 8388608 | bytes 8650752 | tf_op jit(solution)/shard_map/ser,sec->src/dot_general | solution.py:21
  17.6 14.4 %fusion.5 = bf16[128,128,128]{2,1,0:T(8,128)(2,1)S(1)} fusion(s32[128,512]{1,0:T(8,128)S(1)} %get-tuple-element.9, pred[128,512,128]{1,2,0:T(32,128)(4,1)} %iota_compare_fusion.17), kind=kOutput, calls=%fused_computation.8 | convolution fusion | flops 2157969408 | bytes 12845056 | tf_op jit(solution)/shard_map/ser,sec->src/dot_general | solution.py:21
  32.1 2.6 fusion.6
  34.7 0.2 copy.23
  34.9 0.7 copy.15
  35.7 0.1 copy.14
  35.8 0.2 fusion.34
  36.0 8.6 %all_gather.12 = f32[512,256]{1,0:T(8,128)S(1)} all-gather(f32[128,256]{1,0:T(8,128)S(1)} %fusion.34), channel_id=1, replica_groups=mesh['row'=4,'col'=8] {'row'}, dimensions={0}, use_global_device_ids=true | all-gather | bytes 655360 | tf_op jit(solution)/shard_map/all_gather | solution.py:58
  44.6 2.2 fusion.18
  46.9 64.4 %reduce-scatter.5.cloned.1.call-done = f32[128,256]{1,0:T(8,128)} async-done(((f32[1024,256]{1,0:T(8,128)}), f32[128,256]{1,0:T(8,128)}) %reduce-scatter.5.cloned.1.call-update) | async-done | bytes 131088 | tf_op jit(solution)/shard_map/reduce_scatter | solution.py:60
  111.3 1.2 fusion.11
  112.6 5.4 %all_gather.13 = bf16[512,128]{0,1:T(8,128)(2,1)S(1)} all-gather(bf16[128,128]{0,1:T(8,128)(2,1)S(1)} %fusion.11), channel_id=1, replica_groups=mesh['row'=4,'col'=8] {'row'}, dimensions={0}, use_global_device_ids=true | all-gather | bytes 163840 | tf_op jit(solution)/shard_map/all_gather | solution.py:66
  118.0 1.1 fusion.16
  119.1 0.0 reduce-scatter.9.cloned.1.call-start
  119.2 61.5 %reduce-scatter.7.cloned.1.call-done = f32[128,128]{0,1:T(8,128)} async-done(((f32[1024,128]{0,1:T(8,128)}), f32[128,128]{0,1:T(8,128)}) %reduce-scatter.7.cloned.1.call-update) | async-done | bytes 65552 | tf_op jit(solution)/shard_map/reduce_scatter | solution.py:69
  180.7 0.9 select_reduce_fusion
  181.6 0.9 multiply_convert_fusion
  182.5 26.7 %all_gather.14 = bf16[1024,128]{0,1:T(8,128)(2,1)S(1)} all-gather(bf16[128,128]{0,1:T(8,128)(2,1)S(1)} %multiply_convert_fusion), channel_id=1, replica_groups=mesh['row'=4,'col'=8] {'col'}, dimensions={0}, use_global_device_ids=true | all-gather | bytes 294912 | tf_op jit(solution)/shard_map/all_gather | solution.py:38
  209.2 1.2 fusion.14
  210.4 17.7 %reduce-scatter.9.cloned.1.call-done = f32[128,128]{0,1:T(8,128)} async-done(((f32[512,128]{0,1:T(8,128)}), f32[128,128]{0,1:T(8,128)}) %reduce-scatter.9.cloned.1.call-update) | async-done | bytes 65552 | tf_op jit(solution)/shard_map/reduce_scatter | solution.py:42
  228.1 1.2 fusion.10
  229.3 31.4 %all_gather.15 = bf16[1024,256]{1,0:T(8,128)(2,1)S(1)} all-gather(bf16[128,256]{1,0:T(8,128)(2,1)S(1)} %fusion.10), channel_id=1, replica_groups=mesh['row'=4,'col'=8] {'col'}, dimensions={0}, use_global_device_ids=true | all-gather | bytes 589824 | tf_op jit(solution)/shard_map/all_gather | solution.py:38
  260.7 1.2 fusion.12
  262.0 1.8 fusion.29
  263.9 20.0 %reduce-scatter.11.cloned.1.call-done = f32[128,256]{1,0:T(8,128)} async-done(((f32[512,256]{1,0:T(8,128)}), f32[128,256]{1,0:T(8,128)}) %reduce-scatter.11.cloned.1.call-update) | async-done | bytes 131088 | tf_op jit(solution)/shard_map/reduce_scatter | solution.py:42
  283.8 1.8 fusion.24
  285.7 0.6 subtract_reduce_fusion
  286.3 39.5 %psum.23 = f32[]{:T(128)} all-reduce(f32[]{:T(128)} %subtract_reduce_fusion), channel_id=1, replica_groups=mesh['row'=4,'col'=8] {'row','col'}, use_global_device_ids=true, to_apply=%region_9.10 | all-reduce | flops 1 | bytes 8 | tf_op jit(solution)/shard_map/psum | solution.py:105
  326.5 88.7 %all-reduce.3.cloned.1.call-done = (f32[128,256]{1,0:T(8,128)}, f32[256,128]{1,0:T(8,128)}) async-done(((f32[128,256]{1,0:T(8,128)}, f32[256,128]{1,0:T(8,128)}), (f32[128,256]{1,0:T(8,128)}, f32[256,128]{1,0:T(8,128)})) %all-reduce.3.cloned.1.call-update) | async-done | bytes 262160 | tf_op jit(solution)/shard_map/psum | solution.py:105
  415.2 1.6 copy.54
  416.7 1.6 copy.55
  (25 shorter events, 0.3 us)
Async XLA Ops:
  7.2 104.2 %copy-start = (bf16[256,128]{1,0:T(8,128)(2,1)S(1)}, bf16[256,128]{1,0:T(8,128)(2,1)}, u32[]{:S(2)}) copy-start(bf16[256,128]{1,0:T(8,128)(2,1)} %param.11) | copy-start | bytes 196612
  7.2 104.1 %reduce-scatter.5.cloned.1.call-start = ((), (), s32[]{:S(2)}) async-start(), calls=%async_computation.4 | async-start | bytes 1179648 | tf_op jit(solution)/shard_map/reduce_scatter | solution.py:60
  17.6 14.5 %copy-start.6 = (s32[1,128]{1,0:T(1,128)S(1)}, s32[1,128]{1,0:T(1,128)}, u32[]{:S(2)}) copy-start(s32[1,128]{1,0:T(1,128)} %param.13) | copy-start | bytes 1540
  32.0 3.6 copy-start.4
  32.0 3.7 copy-start.2
  32.0 3.7 copy-start.3
  32.1 148.6 %copy-start.5 = (s32[128]{0:T(128)S(1)}, s32[128]{0:T(128)}, u32[]{:S(2)}) copy-start(s32[128]{0:T(128)} %param.12) | copy-start | bytes 1540
  46.9 133.8 %reduce-scatter.7.cloned.1.call-start = ((), (), s32[]{:S(2)}) async-start(), calls=%async_computation.5 | async-start | bytes 589824 | tf_op jit(solution)/shard_map/reduce_scatter | solution.py:69
  111.3 150.7 %copy-start.1 = (f32[128,256]{1,0:T(8,128)S(1)}, f32[128,256]{1,0:T(8,128)}, u32[]{:S(2)}) copy-start(f32[128,256]{1,0:T(8,128)} %reduce-scatter.5.cloned.1.call-done) | copy-start | bytes 393220
  119.1 109.0 %reduce-scatter.9.cloned.1.call-start = ((), (), s32[]{:S(2)}) async-start(), calls=%async_computation.6 | async-start | bytes 327680 | tf_op jit(solution)/shard_map/reduce_scatter | solution.py:42
  210.4 73.5 %reduce-scatter.11.cloned.1.call-start = ((), (), s32[]{:S(2)}) async-start(), calls=%async_computation.7 | async-start | bytes 655360 | tf_op jit(solution)/shard_map/reduce_scatter | solution.py:42
  262.0 153.2 %all-reduce.3.cloned.1.call-start = ((), (), s32[]{:S(2)}) async-start(), calls=%async_computation.8 | async-start | bytes 524288 | tf_op jit(solution)/shard_map/psum | solution.py:105
Sparse Core Ops, SparseCore 0:
  47.0 64.3 reduce-scatter.4
  119.2 61.4 reduce-scatter.6
  210.5 17.5 reduce-scatter.8
  262.1 21.6 reduce-scatter.10
  289.9 125.1 all-reduce.2
where the time goes:
time: 426 us
  waiting for transfers between devices  252 us (59%)
  blocking collectives  112 us (26%)
  matrix products  29 us (7%)
  between operations  16.4 us (4%)
  other arithmetic  10.3 us (2%)
  local copies, waits for them, and re-layouts  6.02 us (1%)
    psum x1, waiting for transfers between devices, per_device(): lax.psum((grad_in_local, grad_out_local, loss_local), ('row', 'col'))  88.7 us
    reduce_scatter x1, waiting for transfers between devices, per_device(): lax.psum_scatter(forward_one, 'col', scatter_dimension=0, tiled=True)  64.4 us
    reduce_scatter x1, waiting for transfers between devices, per_device(): lax.psum_scatter(forward_two, 'col', scatter_dimension=0, tiled=True)  61.5 us
    all_gather x2, blocking collectives, gather_targets(): return lax.all_gather(values, 'col', axis=0, tiled=True)  58.1 us
    psum x1, blocking collectives, per_device(): lax.psum((grad_in_local, grad_out_local, loss_local), ('row', 'col'))  39.5 us
    reduce_scatter x2, waiting for transfers between devices, sum_sources(): lax.psum_scatter(partial_sums, 'row', scatter_dimension=0, tiled=True)  37.7 us
    dot_general x1, matrix products, densify(): jnp.einsum('ser,sec->src', row_onehot, col_onehot, preferred_element_type...  14.4 us
    all_gather x1, blocking collectives, per_device(): gathered_one = lax.all_gather(source_one, 'row', axis=0, tiled=True)  8.65 us
  transfers between devices with their start and end apart: 5, of which 5 were waited for; matrix products, arithmetic and copies ran while one was open for 1% of the time, Pallas kernels for 0%

commit v1 on v0

--- a/solution.py
+++ b/solution.py
@@ -55,7 +55,11 @@
     node_scale = norm_weight[:, None]
     normed = (node_scale * features.astype(jnp.float32)).astype(jnp.bfloat16)
     source_one = jnp.dot(normed, weight_in, preferred_element_type=jnp.float32)
-    gathered_one = lax.all_gather(source_one, "row", axis=0, tiled=True)
+    peers = lax.axis_size("row")
+    repeats = [peers if d == 0 else 1 for d in range(source_one.ndim)]
+    gathered_one = lax.all_to_all(
+        jnp.tile(source_one, repeats), "row", split_axis=0, concat_axis=0, tiled=True
+    )
     forward_one = jnp.dot(adjacency.astype(jnp.float32), gathered_one, precision=HIGHEST)
     projected = lax.psum_scatter(forward_one, "col", scatter_dimension=0, tiled=True)
     pre_hidden = node_scale * (projected + source_one)

time: 426 us -> 426 us (level)
  blocking collectives: 112 us -> 103 us
    all_gather x1 -> x0, blocking collectives: 8.65 us -> none  [per_device(): gathered_one = lax.all_gather(source_one, 'row', axis=0, tiled=True)]
  transfers between devices with their start and end apart: 5 -> 6, of which waited for: 5 -> 5; matrix products, arithmetic and copies ran while one was open for 1% -> 7% of each run, Pallas kernels for 0% -> 0%
where the time goes in v1:
time: 426 us
  waiting for transfers between devices  254 us (60%)
  blocking collectives  103 us (24%)
  matrix products  29.8 us (7%)
  between operations  16.3 us (4%)
  other arithmetic  10.3 us (2%)
  local copies, waits for them, and re-layouts  7.68 us (2%)
  starting transfers between devices  4.41 us (1%)
    psum x1, waiting for transfers between devices, per_device(): lax.psum((grad_in_local, grad_out_local, loss_local), ('row', 'col'))  88.8 us
    reduce_scatter x1, waiting for transfers between devices, per_device(): lax.psum_scatter(forward_one, 'col', scatter_dimension=0, tiled=True)  66 us
    reduce_scatter x1, waiting for transfers between devices, per_device(): lax.psum_scatter(forward_two, 'col', scatter_dimension=0, tiled=True)  61.5 us
    all_gather x2, blocking collectives, gather_targets(): return lax.all_gather(values, 'col', axis=0, tiled=True)  58 us
    psum x1, blocking collectives, per_device(): lax.psum((grad_in_local, grad_out_local, loss_local), ('row', 'col'))  39.5 us
    reduce_scatter x2, waiting for transfers between devices, sum_sources(): lax.psum_scatter(partial_sums, 'row', scatter_dimension=0, tiled=True)  37.7 us
    dot_general x1, matrix products, densify(): jnp.einsum('ser,sec->src', row_onehot, col_onehot, preferred_element_type...  14.4 us
  transfers between devices with their start and end apart: 6, of which 5 were waited for; matrix products, arithmetic and copies ran while one was open for 7% of the time, Pallas kernels for 0%

profile of v1, /device:TPU:0, one launch (start us, length us, event | category | flops | bytes accessed | tf_op | source)
XLA Modules:
  0.0 425.6 jit_solution(10749664166264035728)
XLA Ops:
  7.2 0.9 copy.14
  8.1 1.1 fusion.34
  9.1 0.9 tile.2
  10.0 4.2 all-to-all-start
  14.3 1.7 fusion.37
  16.1 7.9 %iota_compare_fusion.17 = pred[128,512,128]{1,2,0:T(32,128)(4,1)} fusion(s32[128,512]{1,0:T(8,128)S(1)} %get-tuple-element.10), kind=kLoop, calls=%fused_computation.1.clone.clone.clone.clone.2 | loop fusion | flops 8388608 | bytes 8650752 | tf_op jit(solution)/shard_map/ser,sec->src/dot_general | solution.py:21
  24.6 14.4 %fusion.5 = bf16[128,128,128]{2,1,0:T(8,128)(2,1)S(1)} fusion(s32[128,512]{1,0:T(8,128)S(1)} %get-tuple-element.9, pred[128,512,128]{1,2,0:T(32,128)(4,1)} %iota_compare_fusion.17), kind=kOutput, calls=%fused_computation.8 | convolution fusion | flops 2157969408 | bytes 12845056 | tf_op jit(solution)/shard_map/ser,sec->src/dot_general | solution.py:21
  39.1 2.6 fusion.6
  41.7 0.2 copy.23
  41.9 0.7 copy.15
  42.7 2.2 fusion.18
  44.9 66.0 %reduce-scatter.5.cloned.1.call-done = f32[128,256]{1,0:T(8,128)} async-done(((f32[1024,256]{1,0:T(8,128)}), f32[128,256]{1,0:T(8,128)}) %reduce-scatter.5.cloned.1.call-update) | async-done | bytes 131088 | tf_op jit(solution)/shard_map/reduce_scatter | solution.py:64
  110.9 1.2 fusion.11
  112.1 5.4 %all_gather.9 = bf16[512,128]{0,1:T(8,128)(2,1)S(1)} all-gather(bf16[128,128]{0,1:T(8,128)(2,1)S(1)} %fusion.11), channel_id=1, replica_groups=mesh['row'=4,'col'=8] {'row'}, dimensions={0}, use_global_device_ids=true | all-gather | bytes 163840 | tf_op jit(solution)/shard_map/all_gather | solution.py:70
  117.6 1.1 fusion.16
  118.8 61.5 %reduce-scatter.7.cloned.1.call-done = f32[128,128]{0,1:T(8,128)} async-done(((f32[1024,128]{0,1:T(8,128)}), f32[128,128]{0,1:T(8,128)}) %reduce-scatter.7.cloned.1.call-update) | async-done | bytes 65552 | tf_op jit(solution)/shard_map/reduce_scatter | solution.py:73
  180.3 0.9 select_reduce_fusion
  181.2 0.9 multiply_convert_fusion
  182.1 26.6 %all_gather.10 = bf16[1024,128]{0,1:T(8,128)(2,1)S(1)} all-gather(bf16[128,128]{0,1:T(8,128)(2,1)S(1)} %multiply_convert_fusion), channel_id=1, replica_groups=mesh['row'=4,'col'=8] {'col'}, dimensions={0}, use_global_device_ids=true | all-gather | bytes 294912 | tf_op jit(solution)/shard_map/all_gather | solution.py:38
  208.7 1.2 fusion.14
  210.0 17.7 %reduce-scatter.9.cloned.1.call-done = f32[128,128]{0,1:T(8,128)} async-done(((f32[512,128]{0,1:T(8,128)}), f32[128,128]{0,1:T(8,128)}) %reduce-scatter.9.cloned.1.call-update) | async-done | bytes 65552 | tf_op jit(solution)/shard_map/reduce_scatter | solution.py:42
  227.7 1.2 fusion.10
  228.9 31.4 %all_gather.11 = bf16[1024,256]{1,0:T(8,128)(2,1)S(1)} all-gather(bf16[128,256]{1,0:T(8,128)(2,1)S(1)} %fusion.10), channel_id=1, replica_groups=mesh['row'=4,'col'=8] {'col'}, dimensions={0}, use_global_device_ids=true | all-gather | bytes 589824 | tf_op jit(solution)/shard_map/all_gather | solution.py:38
  260.3 1.2 fusion.12
  261.6 1.8 fusion.29
  263.4 20.0 %reduce-scatter.11.cloned.1.call-done = f32[128,256]{1,0:T(8,128)} async-done(((f32[512,256]{1,0:T(8,128)}), f32[128,256]{1,0:T(8,128)}) %reduce-scatter.11.cloned.1.call-update) | async-done | bytes 131088 | tf_op jit(solution)/shard_map/reduce_scatter | solution.py:42
  283.4 1.8 fusion.24
  285.2 0.6 subtract_reduce_fusion
  285.8 39.5 %psum.23 = f32[]{:T(128)} all-reduce(f32[]{:T(128)} %subtract_reduce_fusion), channel_id=1, replica_groups=mesh['row'=4,'col'=8] {'row','col'}, use_global_device_ids=true, to_apply=%region_9.10 | all-reduce | flops 1 | bytes 8 | tf_op jit(solution)/shard_map/psum | solution.py:109
  326.0 88.8 %all-reduce.3.cloned.1.call-done = (f32[128,256]{1,0:T(8,128)}, f32[256,128]{1,0:T(8,128)}) async-done(((f32[128,256]{1,0:T(8,128)}, f32[256,128]{1,0:T(8,128)}), (f32[128,256]{1,0:T(8,128)}, f32[256,128]{1,0:T(8,128)})) %all-reduce.3.cloned.1.call-update) | async-done | bytes 262160 | tf_op jit(solution)/shard_map/psum | solution.py:109
  414.8 1.6 copy.54
  416.4 1.6 copy.55
  (23 shorter events, 0.3 us)
Async XLA Ops:
  7.2 103.7 %copy-start = (bf16[256,128]{1,0:T(8,128)(2,1)S(1)}, bf16[256,128]{1,0:T(8,128)(2,1)}, u32[]{:S(2)}) copy-start(bf16[256,128]{1,0:T(8,128)(2,1)} %param.11) | copy-start | bytes 196612
  10.0 32.6 %all-to-all-start = ((f32[4,128,256]{2,1,0:T(8,128)}), f32[4,128,256]{2,1,0:T(8,128)S(1)}, u32[]{:S(2)}, u32[]{:S(2)}) async-start(f32[4,128,256]{2,1,0:T(8,128)} %tile.2), calls=%async_computation | async-start | bytes 1048576 | tf_op jit(solution)/shard_map/all_to_all | solution.py:60
  14.3 96.6 %reduce-scatter.5.cloned.1.call-start = ((), (), s32[]{:S(2)}) async-start(), calls=%async_computation.5 | async-start | bytes 1179648 | tf_op jit(solution)/shard_map/reduce_scatter | solution.py:64
  24.6 14.5 %copy-start.4 = (s32[1,128]{1,0:T(1,128)S(1)}, s32[1,128]{1,0:T(1,128)}, u32[]{:S(2)}) copy-start(s32[1,128]{1,0:T(1,128)} %param.13) | copy-start | bytes 1540
  39.1 71.9 %copy-start.2 = (f32[128]{0:T(128)S(1)}, f32[128]{0:T(128)}, u32[]{:S(2)}) copy-start(f32[128]{0:T(128)} %param.9) | copy-start | bytes 1540
  39.1 141.2 %copy-start.3 = (s32[128]{0:T(128)S(1)}, s32[128]{0:T(128)}, u32[]{:S(2)}) copy-start(s32[128]{0:T(128)} %param.12) | copy-start | bytes 1540
  44.9 135.4 %reduce-scatter.7.cloned.1.call-start = ((), (), s32[]{:S(2)}) async-start(), calls=%async_computation.6 | async-start | bytes 589824 | tf_op jit(solution)/shard_map/reduce_scatter | solution.py:73
  110.9 150.7 %copy-start.1 = (f32[128,256]{1,0:T(8,128)S(1)}, f32[128,256]{1,0:T(8,128)}, u32[]{:S(2)}) copy-start(f32[128,256]{1,0:T(8,128)} %reduce-scatter.5.cloned.1.call-done) | copy-start | bytes 393220
  118.7 109.0 %reduce-scatter.9.cloned.1.call-start = ((), (), s32[]{:S(2)}) async-start(), calls=%async_computation.7 | async-start | bytes 327680 | tf_op jit(solution)/shard_map/reduce_scatter | solution.py:42
  209.9 73.5 %reduce-scatter.11.cloned.1.call-start = ((), (), s32[]{:S(2)}) async-start(), calls=%async_computation.8 | async-start | bytes 655360 | tf_op jit(solution)/shard_map/reduce_scatter | solution.py:42
  261.6 153.2 %all-reduce.3.cloned.1.call-start = ((), (), s32[]{:S(2)}) async-start(), calls=%async_computation.9 | async-start | bytes 524288 | tf_op jit(solution)/shard_map/psum | solution.py:109
Sparse Core Ops, SparseCore 0:
  45.0 65.8 reduce-scatter.4
  118.8 61.4 reduce-scatter.6
  210.0 17.6 reduce-scatter.8
  261.7 21.6 reduce-scatter.10
  289.5 125.2 all-reduce.2
